TPU v7x, 32 devices: a whole 2x2x4 slice. The times are simulated.
32 devices in a mesh: grp: 2 (over y), exp: 4 (over z), dp: 2 (over x), tp: 2 (over core).
Axes of the slice: x: 2, y: 2, z: 4, core: 2. Of those that a mesh axis runs over, the one named last changes fastest.
Arguments:
- tokens: bfloat16 [1024, 7168], P(('grp', 'exp'), ('dp', 'tp')), parts along dimension 0, may hold values from -6 to 6
- cotangent: bfloat16 [1024, 7168], P(('grp', 'exp'), ('dp', 'tp')), parts along dimension 0, may hold values from -0.1796875 to 0.1796875
- expert_ids: int32 [1024, 2], P(('grp', 'exp')), parts along dimension 0, may hold values from 0 to 3, all different within a row; in each aligned block of 128 rows (0 to 127, 128 to 255, ...) at most 96 rows name the same one
- route_weights: bfloat16 [1024, 2], P(('grp', 'exp')), parts along dimension 0, may hold values from 0.049804688 to 0.59765625
- gate_weight: bfloat16 [8, 7168, 1024], P(('grp', 'exp'), ('dp', 'tp')), parts along dimension 0, may hold values from -0.0625 to 0.0625
- up_weight: bfloat16 [8, 7168, 1024], P(('grp', 'exp'), ('dp', 'tp')), parts along dimension 0, may hold values from -0.0625 to 0.0625
- down_weight: bfloat16 [8, 1024, 7168], P(('grp', 'exp'), None, ('dp', 'tp')), parts along dimension 0, may hold values from -0.1875 to 0.1875
- delta: bfloat16 [8, 1024, 7168], P(('grp', 'exp'), None, ('dp', 'tp')), parts along dimension 0, may hold values from -12 to 12
Outputs:
- grad_down: float32 [8, 1024, 7168], P(('grp', 'exp'), None, ('dp', 'tp')), parts along dimension 0
- unit_scores: float32 [8, 1024], P(('grp', 'exp'), ('dp', 'tp')), parts along dimension 0
- route_grads: float32 [1024, 2], P(('grp', 'exp')), parts along dimension 0
There are 2 independent parts, one for each index of `grp`. A program takes and returns all parts, laid end to end along the dimension named above; each array names one. Nothing has to cross between parts.
Inputs may be any that keep to these rules, and one draw needn't show every extreme that they name: `expert_ids`: each token names 2 different experts. Within the 128 tokens of one index of exp no expert is named more than 96 times, and in every draw some expert is named exactly 96 times by the tokens of some index.
All inputs are finite; a program needn't handle non-finite values.
Results may differ from a plain program's by a relative error of at most 0.018.
Values may be sent and summed in bfloat16 or wider, within the bound.
A program may use at most 128 MiB of HBM per device.

v0:
```python
import jax
import jax.numpy as jnp
from jax import lax
from jax.sharding import PartitionSpec as P

D = 7168


def shards(
    tokens, cotangent, expert_ids, route_weights, gate_weight, up_weight, down_weight, delta
):
    experts = lax.axis_size("exp")
    tok_rows = tokens.shape[0]
    width = tokens.shape[1]
    chosen = expert_ids.shape[1]
    capacity = tok_rows * chosen * 3 // (2 * experts)
    total_rows = experts * capacity
    flat = expert_ids.reshape(-1)
    onehot = (flat[:, None] == jnp.arange(experts, dtype=jnp.int32)[None, :]).astype(jnp.int32)
    earlier = jnp.cumsum(onehot, axis=0) - onehot
    slot = jnp.sum(earlier * onehot, axis=1)
    target = (flat * capacity + slot).reshape(tok_rows, chosen)
    positions = jnp.arange(total_rows, dtype=jnp.int32)
    matches = positions[:, None, None] == target[None, :, :]
    placing = jnp.sum(matches.astype(jnp.float32), axis=2).astype(jnp.bfloat16)
    packed_tokens = jnp.dot(placing, tokens, preferred_element_type=jnp.float32).astype(
        jnp.bfloat16
    )
    packed_cot = jnp.dot(placing, cotangent, preferred_element_type=jnp.float32).astype(
        jnp.bfloat16
    )
    packed_weight = jnp.sum(
        jnp.where(matches, route_weights.astype(jnp.float32)[None, :, :], 0.0), axis=(1, 2)
    ).astype(jnp.bfloat16)
    rows_in, cot_in, weight_in = (
        lax.all_to_all(
            packed_tokens.reshape(experts, capacity, width),
            "exp",
            split_axis=0,
            concat_axis=0,
            tiled=True,
        ),
        lax.all_to_all(
            packed_cot.reshape(experts, capacity, width),
            "exp",
            split_axis=0,
            concat_axis=0,
            tiled=True,
        ),
        lax.all_to_all(
            packed_weight.reshape(experts, capacity), "exp", split_axis=0, concat_axis=0, tiled=True
        ),
    )
    rows_in = rows_in.reshape(total_rows, width)
    cot_in = cot_in.reshape(total_rows, width)
    weight_in = weight_in.reshape(total_rows)
    w_gate = gate_weight[0]
    w_up = up_weight[0]
    w_down = down_weight[0]
    gate_part = jnp.dot(rows_in, w_gate, preferred_element_type=jnp.float32)
    up_part = jnp.dot(rows_in, w_up, preferred_element_type=jnp.float32)
    gate, upper = (
        lax.psum(gate_part.astype(jnp.bfloat16), ("dp", "tp")).astype(jnp.float32),
        lax.psum(up_part.astype(jnp.bfloat16), ("dp", "tp")).astype(jnp.float32),
    )
    hidden = (jax.nn.silu(gate) * upper).astype(jnp.bfloat16)
    outputs = jnp.dot(hidden, w_down, preferred_element_type=jnp.float32)
    returned = lax.all_to_all(
        outputs.reshape(experts, capacity, width).astype(jnp.bfloat16),
        "exp",
        split_axis=0,
        concat_axis=0,
        tiled=True,
    ).astype(jnp.float32)
    picked = jnp.take(returned.reshape(total_rows, width), target.reshape(-1), axis=0).reshape(
        tok_rows, chosen, width
    )
    partial_dots = jnp.sum(picked * cotangent.astype(jnp.float32)[:, None, :], axis=2)
    route_grads = lax.psum(partial_dots, ("dp", "tp"))
    upstream = (weight_in.astype(jnp.float32)[:, None] * cot_in.astype(jnp.float32)).astype(
        jnp.bfloat16
    )
    grad = lax.dot_general(
        hidden, upstream, (((0,), (0,)), ((), ())), preferred_element_type=jnp.float32
    )
    weighted = grad * delta[0].astype(jnp.float32)
    saliency_terms = jnp.sum(weighted * weighted, axis=1)
    unit_totals = lax.psum_scatter(saliency_terms, ("dp", "tp"), scatter_dimension=0, tiled=True)
    unit_scores = jnp.log(unit_totals / D + 1e-06)
    return (grad[None], unit_scores[None], route_grads)


def solution(mesh):
    return jax.shard_map(
        shards,
        mesh=mesh,
        in_specs=(
            P(("grp", "exp"), ("dp", "tp")),
            P(("grp", "exp"), ("dp", "tp")),
            P(("grp", "exp"), None),
            P(("grp", "exp"), None),
            P(("grp", "exp"), ("dp", "tp"), None),
            P(("grp", "exp"), ("dp", "tp"), None),
            P(("grp", "exp"), None, ("dp", "tp")),
            P(("grp", "exp"), None, ("dp", "tp")),
        ),
        out_specs=(
            P(("grp", "exp"), None, ("dp", "tp")),
            P(("grp", "exp"), ("dp", "tp")),
            P(("grp", "exp"), None),
        ),
        check_vma=False,
    )
```

profile of v0, /device:TPU:0, one launch (start us, length us, event | category | flops | bytes accessed | tf_op | source)
XLA Modules:
  0.0 183.9 jit_solution(17395798936894295905)
XLA Ops:
  7.2 0.0 copy-start
  7.2 0.8 copy.30
  8.0 0.1 eq.43
  8.2 0.1 eq.39
  8.3 1.2 reduce-window.6
  9.5 0.1 slice.10
  9.6 0.1 copy.33
  9.8 0.1 copy.34
  9.9 0.1 add_bitcast_fusion
  10.0 0.1 reduce_sum.52
  10.1 0.1 copy.35
  10.2 0.7 convert_element_type.93
  10.9 0.2 select_reduce_fusion
  11.0 0.0 copy-done
  11.0 1.6 convolution_convert_fusion.1
  12.6 6.5 %all-to-all-start = ((bf16[4,96,1792]{2,1,0:T(8,128)(2,1)}), bf16[4,96,1792]{2,1,0:T(8,128)(2,1)S(1)}, u32[]{:S(2)}, u32[]{:S(2)}) async-start(bf16[4,96,1792]{2,1,0:T(8,128)(2,1)} %bitcast.2), calls=%async_computation | async-start | bytes 2752512 | tf_op jit(solution)/shard_map/all_to_all | solution.py:36
  19.1 0.7 convert_element_type.109
  19.7 0.0 copy-done.2
  19.7 1.6 convolution_convert_fusion
  21.3 30.5 %all-to-all-done = bf16[4,96,1792]{2,1,0:T(8,128)(2,1)S(1)} async-done(((bf16[4,96,1792]{2,1,0:T(8,128)(2,1)}), bf16[4,96,1792]{2,1,0:T(8,128)(2,1)S(1)}, u32[]{:S(2)}, u32[]{:S(2)}) %all-to-all-start) | async-done | bytes 1376288 | tf_op jit(solution)/shard_map/all_to_all | solution.py:36
  51.8 3.2 %all-to-all-start.1 = ((bf16[4,1,96]{2,1,0:T(2,128)(2,1)}), bf16[4,1,96]{2,1,0:T(2,128)(2,1)S(1)}, u32[]{:S(2)}, u32[]{:S(2)}) async-start(bf16[4,1,96]{2,1,0:T(2,128)(2,1)} %convert_element_type.109), calls=%async_computation.1 | async-start | bytes 4096 | tf_op jit(solution)/shard_map/all_to_all | solution.py:50
  55.1 4.5 %fusion.17 = bf16[384,1024]{1,0:T(8,128)(2,1)} fusion(bf16[384,1792]{1,0:T(8,128)(2,1)S(1)} %bitcast.63, bf16[1,1792,1024]{2,1,0:T(8,128)(2,1)} %param.12), kind=kOutput, calls=%fused_computation.23 | convolution fusion | flops 1409679360 | bytes 5832704 | tf_op jit(solution)/shard_map/dot_general | solution.py:60
  59.6 0.8 all-to-all-done.1
  60.4 4.2 %all-to-all-start.2 = ((bf16[4,96,1792]{2,1,0:T(8,128)(2,1)}), bf16[4,96,1792]{2,1,0:T(8,128)(2,1)S(1)}, u32[]{:S(2)}, u32[]{:S(2)}) async-start(bf16[4,96,1792]{2,1,0:T(8,128)(2,1)} %bitcast.6), calls=%async_computation.2 | async-start | bytes 2752512 | tf_op jit(solution)/shard_map/all_to_all | solution.py:43
  64.7 4.9 %fusion.20 = bf16[384,1024]{1,0:T(8,128)(2,1)} fusion(bf16[384,1792]{1,0:T(8,128)(2,1)} %bitcast.64, bf16[1,1792,1024]{2,1,0:T(8,128)(2,1)} %param.13), kind=kOutput, calls=%fused_computation.24 | convolution fusion | flops 1409679360 | bytes 5832704 | tf_op jit(solution)/shard_map/dot_general | solution.py:61
  69.6 0.0 all-reduce.5.cloned.1.call-update
  69.6 44.7 %all-reduce.5.cloned.1.call-done = (bf16[384,1024]{1,0:T(8,128)(2,1)}, bf16[384,1024]{1,0:T(8,128)(2,1)}) async-done(((bf16[384,1024]{1,0:T(8,128)(2,1)}, bf16[384,1024]{1,0:T(8,128)(2,1)}), (bf16[384,1024]{1,0:T(8,128)(2,1)}, bf16[384,1024]{1,0:T(8,128)(2,1)})) %all-reduce.5.cloned.1.call-update) | async-done | bytes 1572880 | tf_op jit(solution)/shard_map/psum | solution.py:64
  114.3 1.9 %fusion.16 = bf16[384,1024]{1,0:T(8,128)(2,1)S(1)} fusion(bf16[384,1024]{1,0:T(8,128)(2,1)} %get-tuple-element.16, bf16[384,1024]{1,0:T(8,128)(2,1)} %get-tuple-element.17), kind=kLoop, calls=%fused_computation.22 | loop fusion | flops 3145728 | bytes 2359296 | tf_op jit(solution)/shard_map/convert_element_type | solution.py:66
  116.2 4.7 %fusion.8 = bf16[4,96,1792]{2,1,0:T(8,128)(2,1)} fusion(bf16[4,96,1024]{2,1,0:T(8,128)(2,1)S(1)} %bitcast.62, bf16[1,1024,1792]{2,1,0:T(8,128)(2,1)} %param.14), kind=kOutput, calls=%fused_computation.12 | convolution fusion | flops 1409974272 | bytes 5832704 | tf_op jit(solution)/shard_map/dot_general | solution.py:67
  120.9 0.0 all-to-all-done.2
  120.9 4.6 %all-to-all-start.3 = ((bf16[4,96,1792]{2,1,0:T(8,128)(2,1)}), bf16[4,96,1792]{2,1,0:T(8,128)(2,1)}, u32[]{:S(2)}, u32[]{:S(2)}) async-start(bf16[4,96,1792]{2,1,0:T(8,128)(2,1)} %fusion.8), calls=%async_computation.3 | async-start | bytes 2752512 | tf_op jit(solution)/shard_map/all_to_all | solution.py:68
  125.5 0.1 mul.67
  125.6 0.0 copy-done.1
  125.7 0.1 broadcast_in_dim.39
  125.8 0.5 mul.68
  126.3 0.0 copy-start.4
  126.3 2.5 %mul.69 = f32[256,1792]{1,0:T(8,128)} reshape(f32[128,2,1792]{2,1,0:T(2,128)S(1)} %mul.68) | data formatting | bytes 3670016 | tf_op jit(solution)/shard_map/mul | solution.py:78
  128.8 0.6 dynamic-slice
  130.1 0.1 reshape.140
  130.2 7.9 %fusion.1 = (f32[1024]{0:T(1024)S(1)}, f32[1024,1792]{1,0:T(8,128)}) fusion(bf16[1,1024,1792]{2,1,0:T(8,128)(2,1)} %param.15, bf16[384,1024]{1,0:T(8,128)(2,1)S(1)} %fusion.16, bf16[384,1792]{1,0:T(8,128)(2,1)} %bitcast.61, f32[384]{0:T(512)S(1)} %reshape.140), kind=kOutput, calls=%fused_computation.3 | convolution fusion | flops 1418689536 | bytes 13178368 | tf_op jit(solution)/shard_map/dot_general | solution.py:83
  138.1 20.1 %all-to-all-done.3 = bf16[4,96,1792]{2,1,0:T(8,128)(2,1)} async-done(((bf16[4,96,1792]{2,1,0:T(8,128)(2,1)}), bf16[4,96,1792]{2,1,0:T(8,128)(2,1)}, u32[]{:S(2)}, u32[]{:S(2)}) %all-to-all-start.3) | async-done | bytes 1376288 | tf_op jit(solution)/shard_map/all_to_all | solution.py:68
  158.2 1.5 bitcast_convert_fusion
  159.7 2.6 %gather_fusion = f32[256,1792]{1,0:T(8,128)} fusion(f32[384,1792]{1,0:T(8,128)S(1)} %bitcast_convert_fusion, s32[1024]{0:T(1024)S(1)} %pad_clamp_fusion), kind=kCustom, calls=%fused_computation | custom fusion | bytes 3671040 | tf_op jit(solution)/shard_map/jit(_take)/gather | solution.py:75
  162.3 2.4 %multiply_reduce_fusion = f32[256]{0:T(256)S(1)} fusion(f32[256,1792]{1,0:T(8,128)} %mul.69, f32[256,1792]{1,0:T(8,128)} %gather_fusion, pred[256]{0:T(512)(128)(4,1)S(1)} %broadcast_in_dim.39), kind=kLoop, calls=%fused_computation.17 | loop fusion | flops 1376000 | bytes 3671296 | tf_op jit(solution)/shard_map/reduce_sum | solution.py:78
  164.7 0.1 reduce_sum.58
  164.9 10.9 %all-reduce.1 = (f32[1024]{0:T(1024)S(1)}, f32[128,2]{1,0:T(8,128)S(1)}) all-reduce(f32[1024]{0:T(1024)S(1)} %get-tuple-element.20, f32[128,2]{1,0:T(8,128)S(1)} %reduce_sum.58), channel_id=2, replica_groups=mesh['grp'=2,'exp'=4,'dp'=2,'tp'=2] {'dp','tp'}, use_global_device_ids=true, to_apply=%region_8.9.clone | all-reduce | flops 1280 | bytes 10240
  175.8 0.6 copy.37
  176.4 0.6 fusion.32
  (15 shorter events, 0.1 us)
Async XLA Ops:
  7.2 3.9 %copy-start = (bf16[128,1792]{1,0:T(8,128)(2,1)S(1)}, bf16[128,1792]{1,0:T(8,128)(2,1)}, u32[]{:S(2)}) copy-start(bf16[128,1792]{1,0:T(8,128)(2,1)} %param.8) | copy-start | bytes 1376260
  12.6 7.1 %copy-start.2 = (bf16[128,1792]{1,0:T(8,128)(2,1)S(1)}, bf16[128,1792]{1,0:T(8,128)(2,1)}, u32[]{:S(2)}) copy-start(bf16[128,1792]{1,0:T(8,128)(2,1)} %param.9) | copy-start | bytes 1376260
  12.6 39.2 %all-to-all-start = ((bf16[4,96,1792]{2,1,0:T(8,128)(2,1)}), bf16[4,96,1792]{2,1,0:T(8,128)(2,1)S(1)}, u32[]{:S(2)}, u32[]{:S(2)}) async-start(bf16[4,96,1792]{2,1,0:T(8,128)(2,1)} %bitcast.2), calls=%async_computation | async-start | bytes 2752512 | tf_op jit(solution)/shard_map/all_to_all | solution.py:36
  51.8 7.8 %copy-start.3 = (bf16[4,96,1792]{2,1,0:T(8,128)(2,1)}, bf16[4,96,1792]{2,1,0:T(8,128)(2,1)S(1)}, u32[]{:S(2)}) copy-start(bf16[4,96,1792]{2,1,0:T(8,128)(2,1)S(1)} %all-to-all-done) | copy-start | bytes 4128772
  51.8 8.6 %all-to-all-start.1 = ((bf16[4,1,96]{2,1,0:T(2,128)(2,1)}), bf16[4,1,96]{2,1,0:T(2,128)(2,1)S(1)}, u32[]{:S(2)}, u32[]{:S(2)}) async-start(bf16[4,1,96]{2,1,0:T(2,128)(2,1)} %convert_element_type.109), calls=%async_computation.1 | async-start | bytes 4096 | tf_op jit(solution)/shard_map/all_to_all | solution.py:50
  60.4 60.5 %all-to-all-start.2 = ((bf16[4,96,1792]{2,1,0:T(8,128)(2,1)}), bf16[4,96,1792]{2,1,0:T(8,128)(2,1)S(1)}, u32[]{:S(2)}, u32[]{:S(2)}) async-start(bf16[4,96,1792]{2,1,0:T(8,128)(2,1)} %bitcast.6), calls=%async_computation.2 | async-start | bytes 2752512 | tf_op jit(solution)/shard_map/all_to_all | solution.py:43
  64.7 49.6 %all-reduce.5.cloned.1.call-start = ((), (), s32[]{:S(2)}) async-start(), calls=%async_computation.4 | async-start | bytes 3145728 | tf_op jit(solution)/shard_map/psum | solution.py:64
  120.9 4.7 %copy-start.1 = (bf16[4,96,1792]{2,1,0:T(8,128)(2,1)}, bf16[4,96,1792]{2,1,0:T(8,128)(2,1)S(1)}, u32[]{:S(2)}) copy-start(bf16[4,96,1792]{2,1,0:T(8,128)(2,1)S(1)} %all-to-all-done.2) | copy-start | bytes 4128772
  120.9 37.3 %all-to-all-start.3 = ((bf16[4,96,1792]{2,1,0:T(8,128)(2,1)}), bf16[4,96,1792]{2,1,0:T(8,128)(2,1)}, u32[]{:S(2)}, u32[]{:S(2)}) async-start(bf16[4,96,1792]{2,1,0:T(8,128)(2,1)} %fusion.8), calls=%async_computation.3 | async-start | bytes 2752512 | tf_op jit(solution)/shard_map/all_to_all | solution.py:68
  126.3 2.5 %copy-start.4 = (u32[32]{0:T(128)S(1)}, u32[32]{0:T(128)}, u32[]{:S(2)}) copy-start(u32[32]{0:T(128)} %constant.39) | copy-start | bytes 388
Sparse Core Ops, SparseCore 0:
  69.7 44.5 all-reduce.4
where the time goes:
time: 185 us; the launch traced here: 184 us
  waiting for transfers between devices  96.1 us (52%)
  matrix products  25.3 us (14%)
  starting transfers between devices  18.5 us (10%)
  between operations  14.8 us (8%)
  blocking collectives  10.9 us (6%)
  local copies, waits for them, and re-layouts  9.61 us (5%)
  other arithmetic  8.68 us (5%)
    psum x1, waiting for transfers between devices, shards(): lax.psum(up_part.astype(jnp.bfloat16), ('dp', 'tp')).astype(jnp.float32)  44.7 us
    all_to_all x1, waiting for transfers between devices, shards(): lax.all_to_all(packed_tokens.reshape(experts, capacity, width), 'exp', sp...  30.5 us
    all_to_all x1, waiting for transfers between devices, shards(): lax.all_to_all(outputs.reshape(experts, capacity, width).astype(jnp.bfloa...  20.1 us
    unnamed x1, blocking collectives  10.9 us
    dot_general x1, matrix products, shards(): lax.dot_general(hidden, upstream, (((0,), (0,)), ((), ())), preferred_ele...  7.93 us
    all_to_all x1, starting transfers between devices, shards(): lax.all_to_all(packed_tokens.reshape(experts, capacity, width), 'exp', sp...  6.46 us
    dot_general x1, matrix products, shards(): up_part = jnp.dot(rows_in, w_up, preferred_element_type=jnp.float32)  4.92 us
    dot_general x1, matrix products, shards(): outputs = jnp.dot(hidden, w_down, preferred_element_type=jnp.float32)  4.73 us
  transfers between devices with their start and end apart: 5, of which 4 were waited for; matrix products, arithmetic and copies ran while one was open for 16% of the time, Pallas kernels for 0%

commit v1 on v0

v1 whole, which is shorter than its diff:
```python
import functools

import jax
import jax.numpy as jnp
from jax import lax
from jax.experimental import pallas as pl
from jax.experimental.pallas import tpu as pltpu
from jax.sharding import PartitionSpec as P

MESH = pl.DeviceIdType.MESH
VMEM = pl.BlockSpec(memory_space=pltpu.VMEM)
HBM = pl.BlockSpec(memory_space=pl.ANY)
F32 = jnp.float32
BF16 = jnp.bfloat16


def remote(src, dst, send, recv, **where):
    return pltpu.make_async_remote_copy(
        src_ref=src, dst_ref=dst, send_sem=send, recv_sem=recv,
        device_id=where, device_id_type=MESH,
    )


def greet(n, ndp):
    me, d, t = lax.axis_index("exp"), lax.axis_index("dp"), lax.axis_index("tp")
    return me, d, t


def exchange_kernel(
    n, ndp, nc, cap,
    ids_ref, rw_ref, tok_ref, cot_ref, wg_hbm, wu_hbm,
    hid_ref, cpk_ref, ups_ref, pos_ref,
    wg, wu, meta, full, pk, pp, s1send, s1recv, s1own, s2send, s2recv, s2own, hb,
    wsem, ms, mr, fs, fr, ps, pr, s1s, s1r, s2s, s2r, hs, hr, ts, tr,
):
    me, d, t = lax.axis_index("exp"), lax.axis_index("dp"), lax.axis_index("tp")
    pairs = n // 2
    q, b = me // 2, me % 2
    mate = q * 2 + (1 - b)
    other = 1 - t
    rows, width = tok_ref.shape
    wc = width // nc
    ff = wg.shape[1]
    half = ff // 2
    part = half // ndp
    srcs = (tok_ref, cot_ref)
    group_rows = 2 * cap

    loads = [pltpu.make_async_copy(wg_hbm.at[0], wg, wsem.at[0]),
             pltpu.make_async_copy(wu_hbm.at[0], wu, wsem.at[1])]
    for load in loads:
        load.start()

    barrier = pltpu.get_barrier_semaphore()
    for i in range(1, n):
        pl.semaphore_signal(barrier, inc=1, device_id={"exp": lax.rem(me + i, n)}, device_id_type=MESH)
    for i in range(1, ndp):
        pl.semaphore_signal(barrier, inc=1, device_id={"dp": lax.rem(d + i, ndp)}, device_id_type=MESH)
    pl.semaphore_signal(barrier, inc=1, device_id={"tp": other}, device_id_type=MESH)

    ne = max(n, 16)
    expert = lax.broadcasted_iota(jnp.int32, (ne, rows), 0)
    named = jnp.zeros((ne, rows), F32)
    share = jnp.zeros((ne, rows), F32)
    for k in range(ids_ref.shape[0]):
        hit = expert == ids_ref[k:k + 1, :]
        named = named + jnp.where(hit, 1.0, 0.0)
        share = share + jnp.where(hit, rw_ref[k:k + 1, :], 0.0)
    before = (lax.broadcasted_iota(jnp.int32, (rows, rows), 0)
              < lax.broadcasted_iota(jnp.int32, (rows, rows), 1))
    count = jnp.dot(named.astype(BF16), jnp.where(before, 1.0, 0.0).astype(BF16),
                    preferred_element_type=F32)
    place = jnp.where(named > 0.5, count, -1.0)
    for e in range(n):
        meta[me, e, 0:1, :] = place[e:e + 1, :]
        meta[me, e, 1:2, :] = share[e:e + 1, :]
        meta[me, e, 2:8, :] = jnp.zeros((6, rows), F32)

    pl.semaphore_wait(barrier, n - 1 + ndp)

    slot_iota = lax.broadcasted_iota(jnp.int32, (cap, rows), 0).astype(F32)

    def placing(s, e):
        return jnp.where(meta[s, e, 0:1, :] == slot_iota, 1.0, 0.0).astype(BF16)

    def cols(c):
        return slice(c * wc, (c + 1) * wc)

    def meta_copy(to):
        pair = pl.ds(2 * (to // 2), 2)
        return remote(meta.at[me, pair], meta.at[me, pair], ms.at[to], mr.at[me], exp=to)

    def meta_arrive(s):
        pair = pl.ds(2 * q, 2)
        return remote(meta.at[s, pair], meta.at[s, pair], ms.at[s], mr.at[s], exp=s)

    def full_copy(a, p, c):
        to = 2 * p + jnp.where(p > q, 0, 1)
        return remote(srcs[a].at[:, cols(c)], full.at[a, me, :, cols(c)],
                      fs.at[a, p, c], fr.at[a, me, c], exp=to)

    def full_arrive(a, s, c):
        return remote(srcs[a].at[:, cols(c)], full.at[a, s, :, cols(c)],
                      fs.at[a, q, c], fr.at[a, s, c], exp=mate)

    def pack_copy(a, s, c):
        return remote(pp.at[a, s, :, cols(c)], pk.at[a, s, :, cols(c)],
                      ps.at[a, s, c], pr.at[a, s, c], exp=mate)

    def own_sends(a):
        for c in range(nc):
            for g in range(1, pairs):
                full_copy(a, lax.rem(q + g, pairs), c).start()
        to_mate = placing(me, mate)
        for c in range(nc):
            pp[a, me, :, cols(c)] = jnp.dot(
                to_mate, srcs[a][:, cols(c)], preferred_element_type=F32).astype(BF16)
            pack_copy(a, me, c).start()
        mine = placing(me, me)
        for c in range(nc):
            pk[a, me, :, cols(c)] = jnp.dot(
                mine, srcs[a][:, cols(c)], preferred_element_type=F32).astype(BF16)

    def own_sent(a):
        for g in range(1, pairs):
            for c in range(nc):
                full_copy(a, lax.rem(q + g, pairs), c).wait_send()
        for c in range(nc):
            pack_copy(a, me, c).wait_send()

    def is_near(p):
        return ((p < q) & (b == 0)) | ((p > q) & (b == 1))

    def relay(a, g, c):
        p = lax.rem(q + g, pairs)

        @pl.when(is_near(p))
        def _():
            for j in range(2):
                s = 2 * p + j
                full_arrive(a, s, c).wait_recv()
                block = full[a, s, :, cols(c)]
                pp[a, s, :, cols(c)] = jnp.dot(
                    placing(s, mate), block, preferred_element_type=F32).astype(BF16)
                pack_copy(a, s, c).start()
                pk[a, s, :, cols(c)] = jnp.dot(
                    placing(s, me), block, preferred_element_type=F32).astype(BF16)

    def arrived(a, g):
        p = lax.rem(q + g, pairs)
        if g == 0:
            for c in range(nc):
                pack_copy(a, mate, c).wait_recv()
        else:
            @pl.when(jnp.logical_not(is_near(p)))
            def _():
                for j in range(2):
                    for c in range(nc):
                        pack_copy(a, 2 * p + j, c).wait_recv()

    def s1_copy(g):
        return remote(s1send.at[g], s1recv.at[g], s1s.at[g], s1r.at[g], tp=other)

    def s2_copy(g, to):
        return remote(s2send.at[g, to], s2recv.at[g, d], s2s.at[g, to], s2r.at[g, d], dp=to)

    def s2_arrive(g, frm):
        return remote(s2send.at[g, frm], s2recv.at[g, frm], s2s.at[g, frm], s2r.at[g, frm], dp=frm)

    def h_copy(g, to):
        return remote(hb.at[g, t, d], hb.at[g, t, d], hs.at[g, to], hr.at[g, d], dp=to)

    def h_arrive(g, frm):
        return remote(hb.at[g, t, frm], hb.at[g, t, frm], hs.at[g, frm], hr.at[g, frm], dp=frm)

    def t_copy(g, i):
        return remote(hb.at[g, t, i], hb.at[g, t, i], ts.at[g, i], tr.at[g, i], tp=other)

    def t_arrive(g, i):
        return remote(hb.at[g, other, i], hb.at[g, other, i], ts.at[g, i], tr.at[g, i], tp=other)

    tile = min(256, half)

    def products(g):
        p = lax.rem(q + g, pairs)

        def into(target, side):
            @pl.loop(0, half // tile)
            def _(i):
                x = pk[0, pl.ds(2 * p, 2)].reshape(group_rows, width)
                at = pl.ds(pl.multiple_of(side * half + i * tile, tile), tile)
                put = pl.ds(pl.multiple_of(i * tile, tile), tile)
                target[g, 0, :, put] = jnp.dot(x, wg[:, at], preferred_element_type=F32).astype(BF16)
                target[g, 1, :, put] = jnp.dot(x, wu[:, at], preferred_element_type=F32).astype(BF16)

        into(s1send, other)
        s1_copy(g).start()
        into(s1own, t)

    def sums(g):
        s1_copy(g).wait_recv()
        for i in range(ndp):
            at = slice(i * part, (i + 1) * part)
            total = s1own[g, :, :, at].astype(F32) + s1recv[g, :, :, at].astype(F32)
            s2send[g, i] = total.astype(BF16)

            @pl.when(d == i)
            def _():
                s2own[g] = total
        for i in range(1, ndp):
            s2_copy(g, lax.rem(d + i, ndp)).start()

    def activate(g):
        total = s2own[g]
        for i in range(1, ndp):
            frm = lax.rem(d + i, ndp)
            s2_arrive(g, frm).wait_recv()
            total = total + s2recv[g, frm].astype(F32)
        gate, upper = total[0], total[1]
        hb[g, t, d] = (gate / (1.0 + jnp.exp(-gate)) * upper).astype(BF16)
        for i in range(1, ndp):
            h_copy(g, lax.rem(d + i, ndp)).start()
        t_copy(g, d).start()

    def forward(g):
        for i in range(1, ndp):
            frm = lax.rem(d + i, ndp)
            h_arrive(g, frm).wait_recv()
            t_copy(g, frm).start()

    def finish(g):
        p = lax.rem(q + g, pairs)
        for i in range(ndp):
            t_arrive(g, i).wait_recv()
        for side in range(2):
            for i in range(ndp):
                at = side * half + i * part
                hid_ref[p, :, at:at + part] = hb[g, side, i]

    def upstream(g):
        p = lax.rem(q + g, pairs)
        for j in range(2):
            s = 2 * p + j
            spread = jnp.where(meta[s, me, 0:1, :] == slot_iota, meta[s, me, 1:2, :], 0.0)
            scale = jnp.sum(spread, axis=1, keepdims=True)
            block = pk[1, s]
            cpk_ref[s] = block
            ups_ref[s] = (scale * block.astype(F32)).astype(BF16)

    for i in range(1, n):
        meta_copy(lax.rem(me + i, n)).start()
    own_sends(0)
    for i in range(1, n):
        meta_arrive(lax.rem(me + i, n)).wait_recv()
    for s in range(n):
        pos_ref[s] = meta[s, me, 0:1, :]

    for g in range(1, pairs):
        for c in range(nc - 1):
            relay(0, g, c)
    for load in loads:
        load.wait()
    arrived(0, 0)
    products(0)
    sums(0)
    for g in range(1, pairs):
        relay(0, g, nc - 1)
    own_sent(0)
    own_sends(1)
    activate(0)
    forward(0)
    for g in range(1, pairs):
        arrived(0, g)
        products(g)
        sums(g)
    finish(0)
    for g in range(1, pairs):
        for c in range(nc - 1):
            relay(1, g, c)
    for g in range(1, pairs):
        activate(g)
    for g in range(1, pairs):
        forward(g)
    for g in range(1, pairs):
        finish(g)
    arrived(1, 0)
    upstream(0)
    for g in range(1, pairs):
        relay(1, g, nc - 1)
    for g in range(1, pairs):
        arrived(1, g)
        upstream(g)

    for i in range(1, n):
        meta_copy(lax.rem(me + i, n)).wait_send()
    own_sent(1)
    for g in range(pairs):
        s1_copy(g).wait_send()
        for i in range(1, ndp):
            s2_copy(g, lax.rem(d + i, ndp)).wait_send()
            h_copy(g, lax.rem(d + i, ndp)).wait_send()
        for i in range(ndp):
            t_copy(g, i).wait_send()
        if g:
            p = lax.rem(q + g, pairs)

            @pl.when(is_near(p))
            def _():
                for a in range(2):
                    for j in range(2):
                        for c in range(nc):
                            pack_copy(a, 2 * p + j, c).wait_send()


def gradient_kernel(n, cap, tile, hid_ref, ups_ref, cpk_ref, pos_ref, wd_ref, delta_ref,
                    grad_ref, stat_ref, dots):
    step = pl.program_id(0)
    h = hid_ref[...]
    grad = lax.dot_general(h, ups_ref[...], (((0,), (0,)), ((), ())), preferred_element_type=F32)
    grad_ref[0] = grad
    term = grad * delta_ref[0].astype(F32)
    term = term * term
    lanes = term[:, 0:128]
    for i in range(1, term.shape[1] // 128):
        lanes = lanes + term[:, i * 128:(i + 1) * 128]
    for i in range(tile // 128):
        stat_ref[n + step * (tile // 128) + i] = jnp.sum(
            lanes[i * 128:(i + 1) * 128, :].T, axis=0, keepdims=True)
    back = lax.dot_general(cpk_ref[...], wd_ref[0], (((1,), (1,)), ((), ())), preferred_element_type=F32)
    inner = jnp.sum(back * h.astype(F32), axis=1, keepdims=True)

    @pl.when(step == 0)
    def _():
        dots[...] = inner

    @pl.when(step > 0)
    def _():
        dots[...] += inner

    @pl.when(step == pl.num_programs(0) - 1)
    def _():
        slot = lax.broadcasted_iota(jnp.int32, (cap, 128), 0).astype(F32)
        for s in range(n):
            mine = jnp.where(pos_ref[s] == slot, dots[s * cap:(s + 1) * cap, :], 0.0)
            stat_ref[s] = jnp.sum(mine, axis=0, keepdims=True)


def reduce_kernel(n, ndp, features, stat_ref, ids_ref, unit_ref, route_ref,
                  got, total, back, gs, gr, bs, br):
    me, d, t = lax.axis_index("exp"), lax.axis_index("dp"), lax.axis_index("tp")
    own = d * 2 + t
    peers = 2 * ndp
    barrier = pltpu.get_barrier_semaphore()

    def peer(i):
        to = lax.rem(own + i, peers)
        return to, {"dp": to // 2, "tp": lax.rem(to, 2)}

    for i in range(1, peers):
        pl.semaphore_signal(barrier, inc=1, device_id=peer(i)[1], device_id_type=MESH)
    for i in range(1, n):
        pl.semaphore_signal(barrier, inc=1, device_id={"exp": lax.rem(me + i, n)}, device_id_type=MESH)
    pl.semaphore_wait(barrier, peers - 1 + n - 1)

    def gather(i):
        to, where = peer(i)
        return remote(stat_ref, got.at[own], gs.at[to], gr.at[own], **where)

    def gathered(i):
        frm, where = peer(i)
        return remote(stat_ref, got.at[frm], gs.at[frm], gr.at[frm], **where)

    for i in range(1, peers):
        gather(i).start()
    got[own] = stat_ref[...]
    for i in range(1, peers):
        gathered(i).wait_recv()
    added = got[0]
    for i in range(1, peers):
        added = added + got[i]
    total[...] = added

    def give(to):
        return remote(total.at[to], back.at[me], bs.at[to], br.at[me], exp=to)

    def given(frm):
        return remote(total.at[frm], back.at[frm], bs.at[frm], br.at[frm], exp=frm)

    for i in range(1, n):
        give(lax.rem(me + i, n)).start()
    back[me] = total[me]
    units = unit_ref.shape[0]
    unit_ref[...] = jnp.log(total[pl.ds(n + own * units, units)] / features + 1e-6)
    for i in range(1, n):
        given(lax.rem(me + i, n)).wait_recv()
    for k in range(ids_ref.shape[0]):
        chosen = ids_ref[k:k + 1, :]
        picked = jnp.zeros(chosen.shape, F32)
        for e in range(n):
            picked = picked + jnp.where(chosen == e, back[e], 0.0)
        route_ref[k:k + 1, :] = picked
    for i in range(1, peers):
        gather(i).wait_send()
    for i in range(1, n):
        give(lax.rem(me + i, n)).wait_send()


def shards(tokens, cotangent, expert_ids, route_weights, gate_weight, up_weight, down_weight, delta):
    n, ndp = lax.axis_size("exp"), lax.axis_size("dp")
    rows, width = tokens.shape
    chosen = expert_ids.shape[1]
    cap = rows * chosen * 3 // (2 * n)
    total = n * cap
    ff = gate_weight.shape[2]
    half, pairs = ff // 2, n // 2
    part = half // ndp
    nc = 2 if width % 256 == 0 else 1
    ids = expert_ids.T
    shares = route_weights.T.astype(F32)
    dma = pltpu.SemaphoreType.DMA
    hidden, cpk, ups, pos = pl.pallas_call(
        functools.partial(exchange_kernel, n, ndp, nc, cap),
        out_shape=(
            jax.ShapeDtypeStruct((pairs, 2 * cap, ff), BF16),
            jax.ShapeDtypeStruct((n, cap, width), BF16),
            jax.ShapeDtypeStruct((n, cap, width), BF16),
            jax.ShapeDtypeStruct((n, 1, rows), F32),
        ),
        in_specs=[VMEM, VMEM, VMEM, VMEM, HBM, HBM],
        out_specs=(VMEM, VMEM, VMEM, VMEM),
        scratch_shapes=[
            pltpu.VMEM((width, ff), BF16),
            pltpu.VMEM((width, ff), BF16),
            pltpu.VMEM((n, n, 8, rows), F32),
            pltpu.VMEM((2, n, rows, width), BF16),
            pltpu.VMEM((2, n, cap, width), BF16),
            pltpu.VMEM((2, n, cap, width), BF16),
            pltpu.VMEM((pairs, 2, 2 * cap, half), BF16),
            pltpu.VMEM((pairs, 2, 2 * cap, half), BF16),
            pltpu.VMEM((pairs, 2, 2 * cap, half), BF16),
            pltpu.VMEM((pairs, ndp, 2, 2 * cap, part), BF16),
            pltpu.VMEM((pairs, ndp, 2, 2 * cap, part), BF16),
            pltpu.VMEM((pairs, 2, 2 * cap, part), F32),
            pltpu.VMEM((pairs, 2, ndp, 2 * cap, part), BF16),
            dma((2,)), dma((n,)), dma((n,)),
            dma((2, pairs, nc)), dma((2, n, nc)), dma((2, n, nc)), dma((2, n, nc)),
            dma((pairs,)), dma((pairs,)),
            dma((pairs, ndp)), dma((pairs, ndp)),
            dma((pairs, ndp)), dma((pairs, ndp)),
            dma((pairs, ndp)), dma((pairs, ndp)),
        ],
        compiler_params=pltpu.CompilerParams(
            collective_id=0, has_side_effects=True, vmem_limit_bytes=60 * 2**20),
        name="exchange",
    )(ids, shares, tokens, cotangent, gate_weight, up_weight)

    tile = 256
    stats = n + ff // 128
    whole = lambda shape: pl.BlockSpec(shape, lambda i: (0,) * len(shape))
    grad, stat = pl.pallas_call(
        functools.partial(gradient_kernel, n, cap, tile),
        grid=(ff // tile,),
        out_shape=(
            jax.ShapeDtypeStruct((1, ff, width), F32),
            jax.ShapeDtypeStruct((stats, 1, 128), F32),
        ),
        in_specs=[
            pl.BlockSpec((total, tile), lambda i: (0, i)),
            whole((total, width)),
            whole((total, width)),
            whole((n, 1, rows)),
            pl.BlockSpec((1, tile, width), lambda i: (0, i, 0)),
            pl.BlockSpec((1, tile, width), lambda i: (0, i, 0)),
        ],
        out_specs=(
            pl.BlockSpec((1, tile, width), lambda i: (0, i, 0)),
            whole((stats, 1, 128)),
        ),
        scratch_shapes=[pltpu.VMEM((total, 1), F32)],
        compiler_params=pltpu.CompilerParams(vmem_limit_bytes=56 * 2**20),
        name="gradient",
    )(hidden.reshape(total, ff), ups.reshape(total, width), cpk.reshape(total, width),
      pos, down_weight, delta)

    units = ff // (2 * ndp) // 128
    unit, route = pl.pallas_call(
        functools.partial(reduce_kernel, n, ndp, float(width * 2 * ndp)),
        out_shape=(
            jax.ShapeDtypeStruct((units, 1, 128), F32),
            jax.ShapeDtypeStruct((chosen, rows), F32),
        ),
        in_specs=[VMEM, VMEM],
        out_specs=(VMEM, VMEM),
        scratch_shapes=[
            pltpu.VMEM((2 * ndp, stats, 1, 128), F32),
            pltpu.VMEM((stats, 1, 128), F32),
            pltpu.VMEM((n, 1, 128), F32),
            dma((2 * ndp,)), dma((2 * ndp,)), dma((n,)), dma((n,)),
        ],
        compiler_params=pltpu.CompilerParams(collective_id=1, has_side_effects=True),
        name="reduce",
    )(stat, ids)
    return grad, unit.reshape(1, units * 128), route.T


def solution(mesh):
    return jax.shard_map(
        shards,
        mesh=mesh,
        in_specs=(
            P(("grp", "exp"), ("dp", "tp")),
            P(("grp", "exp"), ("dp", "tp")),
            P(("grp", "exp"), None),
            P(("grp", "exp"), None),
            P(("grp", "exp"), ("dp", "tp"), None),
            P(("grp", "exp"), ("dp", "tp"), None),
            P(("grp", "exp"), None, ("dp", "tp")),
            P(("grp", "exp"), None, ("dp", "tp")),
        ),
        out_specs=(
            P(("grp", "exp"), None, ("dp", "tp")),
            P(("grp", "exp"), ("dp", "tp")),
            P(("grp", "exp"), None),
        ),
        check_vma=False,
    )
```

time: 185 us -> 95.3 us (0.52)
  waiting for transfers between devices: 96.1 us -> 0 us
  Pallas kernels: 0 us -> 90.7 us
  matrix products: 25.3 us -> 0 us
  starting transfers between devices: 18.5 us -> 0 us
  between operations: 14.8 us -> 0.65 us
  blocking collectives: 10.9 us -> 0 us
  other arithmetic: 8.68 us -> 1.22 us
  local copies, waits for them, and re-layouts: 9.61 us -> 2.43 us
    pallas_call x0 -> x3, Pallas kernels: none -> 90.7 us  [the longest x1 69.1 us: shards(): pl.pallas_call(functools.partial(exchange_kernel, n, ndp, nc, cap), out_s...]
    all_to_all x4 -> x0, waiting for transfers between devices: 51.4 us -> none  [the longest x1 30.5 us: shards(): lax.all_to_all(packed_tokens.reshape(experts, capacity, width), 'exp', sp...]
    psum x1 -> x0, waiting for transfers between devices: 44.7 us -> none  [shards(): lax.psum(up_part.astype(jnp.bfloat16), ('dp', 'tp')).astype(jnp.float32)]
    dot_general x6 -> x0, matrix products: 25.3 us -> none  [the longest x1 7.93 us: shards(): lax.dot_general(hidden, upstream, (((0,), (0,)), ((), ())), preferred_ele...]
    all_to_all x4 -> x0, starting transfers between devices: 18.5 us -> none  [the longest x1 6.46 us: shards(): lax.all_to_all(packed_tokens.reshape(experts, capacity, width), 'exp', sp...]
    unnamed x1 -> x0, blocking collectives: 10.9 us -> none
    mul x3 -> x0, local copies, waits for them, and re-layouts: 3.12 us -> none  [the longest x2 2.99 us: shards(): picked * cotangent.astype(jnp.float32)[:, None, :]]
    gather x1 -> x0, local copies, waits for them, and re-layouts: 2.62 us -> none  [shards(): jnp.take(returned.reshape(total_rows, width), target.reshape(-1), axis=0)]
  transfers between devices with their start and end apart: 5 -> 0, of which waited for: 4 -> 0; matrix products, arithmetic and copies ran while one was open for 16% -> 0% of each run, Pallas kernels for 0% -> 0%
where the time goes in v1:
time: 95.3 us; the launch traced here: 95 us
  Pallas kernels  90.7 us (95%)
  local copies, waits for them, and re-layouts  2.43 us (3%)
  other arithmetic  1.22 us (1%)
    pallas_call x1, Pallas kernels, shards(): pl.pallas_call(functools.partial(exchange_kernel, n, ndp, nc, cap), out_s...  69.1 us
    pallas_call x1, Pallas kernels, shards(): pl.pallas_call(functools.partial(reduce_kernel, n, ndp, float(width * 2 *...  11.7 us
    pallas_call x1, Pallas kernels, shards(): pl.pallas_call(functools.partial(gradient_kernel, n, cap, tile), grid=(ff...  9.94 us
    unnamed x2, local copies, waits for them, and re-layouts  2.43 us

profile of v1, /device:TPU:0, one launch (start us, length us, event | category | flops | bytes accessed | tf_op | source)
XLA Modules:
  0.0 95.0 jit_solution(506387092213137636)
XLA Ops:
  0.6 1.2 %convert_bitcast_fusion.rw_ref = f32[2,128]{1,0:T(2,128)} fusion(bf16[128,2]{0,1:T(2,128)(2,1)} %param.11), kind=kLoop, calls=%fused_computation | loop fusion | flops 256 | bytes 1536 | tf_op jit(solution)/shard_map/convert_element_type | solution.py:419
  1.8 69.1 %exchange.1 = (bf16[2,192,1024]{2,1,0:T(8,128)(2,1)}, bf16[4,96,1792]{2,1,0:T(8,128)(2,1)}, bf16[4,96,1792]{2,1,0:T(8,128)(2,1)}, f32[4,1,128]{2,1,0:T(1,128)}) custom-call(s32[2,128]{1,0:T(2,128)} %bitcast.11, f32[2,128]{1,0:T(2,128)} %convert_bitcast_fusion.rw_ref, bf16[128,1792]{1,0:T(8,128)(2,1)} %tok_ref.1, bf16[128,1792]{1,0:T(8,128)(2,1)} %cot_ref.1, ...), custom_call_target="tpu_custom_call" | custom-call | tf_op jit(solution)/shard_map/exchange/pallas_call | solution.py:421
  70.9 9.9 %gradient.1 = (f32[1,1024,1792]{2,1,0:T(8,128)}, f32[12,1,128]{2,1,0:T(1,128)}) custom-call(bf16[384,1024]{1,0:T(8,128)(2,1)} %bitcast.10, bf16[384,1792]{1,0:T(8,128)(2,1)} %bitcast.9, bf16[384,1792]{1,0:T(8,128)(2,1)} %bitcast.8, f32[4,1,128]{2,1,0:T(1,128)} %get-tuple-element.14.pos_ref, bf16[1,1024,1792]{2,1,0:T(8,128)(2,1)} %wd_ref.1, ...), custom_call_target="tpu_custom_call" | custom-call | tf_op jit(solution)/shard_map/gradient/pallas_call | solution.py:460
  80.9 11.7 %reduce.1 = (f32[2,1,128]{2,1,0:T(1,128)}, f32[2,128]{1,0:T(2,128)}) custom-call(f32[12,1,128]{2,1,0:T(1,128)} %get-tuple-element.16.stat_ref, s32[2,128]{1,0:T(2,128)} %bitcast.12), custom_call_target="tpu_custom_call" | custom-call | tf_op jit(solution)/shard_map/reduce/pallas_call | solution.py:486
  92.6 1.2 %copy.13 = f32[1,256]{1,0:T(1,128)} copy(f32[1,256]{1,0:T(1,128)} %bitcast.14) | data formatting | bytes 2048
  93.8 1.2 %copy.14 = f32[128,2]{0,1:T(2,128)} copy(f32[128,2]{0,1:T(2,128)} %bitcast.13) | data formatting | bytes 2048

commit v2 on v1

--- a/solution.py
+++ b/solution.py
@@ -21,16 +21,11 @@
     )
 
 
-def greet(n, ndp):
-    me, d, t = lax.axis_index("exp"), lax.axis_index("dp"), lax.axis_index("tp")
-    return me, d, t
-
-
 def exchange_kernel(
-    n, ndp, nc, cap,
-    ids_ref, rw_ref, tok_ref, cot_ref, wg_hbm, wu_hbm,
-    hid_ref, cpk_ref, ups_ref, pos_ref,
-    wg, wu, meta, full, pk, pp, s1send, s1recv, s1own, s2send, s2recv, s2own, hb,
+    n, ndp, edges, cap,
+    ids_ref, rw_ref, tok_ref, cot_ref, wg_hbm, wu_hbm, wd_hbm,
+    hid_ref, ups_ref, dots_ref,
+    wg, wu, wd, meta, full, pk, pp, s1send, s1recv, s1own, s2send, s2recv, s2own, hb,
     wsem, ms, mr, fs, fr, ps, pr, s1s, s1r, s2s, s2r, hs, hr, ts, tr,
 ):
     me, d, t = lax.axis_index("exp"), lax.axis_index("dp"), lax.axis_index("tp")
@@ -39,7 +34,7 @@
     mate = q * 2 + (1 - b)
     other = 1 - t
     rows, width = tok_ref.shape
-    wc = width // nc
+    nc = len(edges) - 1
     ff = wg.shape[1]
     half = ff // 2
     part = half // ndp
@@ -47,7 +42,8 @@
     group_rows = 2 * cap
 
     loads = [pltpu.make_async_copy(wg_hbm.at[0], wg, wsem.at[0]),
-             pltpu.make_async_copy(wu_hbm.at[0], wu, wsem.at[1])]
+             pltpu.make_async_copy(wu_hbm.at[0], wu, wsem.at[1]),
+             pltpu.make_async_copy(wd_hbm.at[0], wd, wsem.at[2])]
     for load in loads:
         load.start()
 
@@ -65,7 +61,7 @@
     for k in range(ids_ref.shape[0]):
         hit = expert == ids_ref[k:k + 1, :]
         named = named + jnp.where(hit, 1.0, 0.0)
-        share = share + jnp.where(hit, rw_ref[k:k + 1, :], 0.0)
+        share = share + jnp.where(hit, rw_ref[k:k + 1, :].astype(F32), 0.0)
     before = (lax.broadcasted_iota(jnp.int32, (rows, rows), 0)
               < lax.broadcasted_iota(jnp.int32, (rows, rows), 1))
     count = jnp.dot(named.astype(BF16), jnp.where(before, 1.0, 0.0).astype(BF16),
@@ -84,7 +80,7 @@
         return jnp.where(meta[s, e, 0:1, :] == slot_iota, 1.0, 0.0).astype(BF16)
 
     def cols(c):
-        return slice(c * wc, (c + 1) * wc)
+        return slice(edges[c], edges[c + 1])
 
     def meta_copy(to):
         pair = pl.ds(2 * (to // 2), 2)
@@ -107,19 +103,22 @@
         return remote(pp.at[a, s, :, cols(c)], pk.at[a, s, :, cols(c)],
                       ps.at[a, s, c], pr.at[a, s, c], exp=mate)
 
+    def placing_both(s):
+        return jnp.concatenate([placing(s, mate), placing(s, me)], axis=0)
+
+    def pack(a, s, c, both, block):
+        packed = jnp.dot(both, block, preferred_element_type=F32).astype(BF16)
+        pp[a, s, :, cols(c)] = packed[:cap]
+        pack_copy(a, s, c).start()
+        pk[a, s, :, cols(c)] = packed[cap:]
+
     def own_sends(a):
         for c in range(nc):
             for g in range(1, pairs):
                 full_copy(a, lax.rem(q + g, pairs), c).start()
-        to_mate = placing(me, mate)
+        both = placing_both(me)
         for c in range(nc):
-            pp[a, me, :, cols(c)] = jnp.dot(
-                to_mate, srcs[a][:, cols(c)], preferred_element_type=F32).astype(BF16)
-            pack_copy(a, me, c).start()
-        mine = placing(me, me)
-        for c in range(nc):
-            pk[a, me, :, cols(c)] = jnp.dot(
-                mine, srcs[a][:, cols(c)], preferred_element_type=F32).astype(BF16)
+            pack(a, me, c, both, srcs[a][:, cols(c)])
 
     def own_sent(a):
         for g in range(1, pairs):
@@ -139,12 +138,7 @@
             for j in range(2):
                 s = 2 * p + j
                 full_arrive(a, s, c).wait_recv()
-                block = full[a, s, :, cols(c)]
-                pp[a, s, :, cols(c)] = jnp.dot(
-                    placing(s, mate), block, preferred_element_type=F32).astype(BF16)
-                pack_copy(a, s, c).start()
-                pk[a, s, :, cols(c)] = jnp.dot(
-                    placing(s, me), block, preferred_element_type=F32).astype(BF16)
+                pack(a, s, c, placing_both(s), full[a, s, :, cols(c)])
 
     def arrived(a, g):
         p = lax.rem(q + g, pairs)
@@ -239,60 +233,76 @@
 
     def upstream(g):
         p = lax.rem(q + g, pairs)
+        step = min(256, ff)
+
+        def inner(i, acc):
+            at = pl.ds(pl.multiple_of(i * step, step), step)
+            x = pk[1, pl.ds(2 * p, 2)].reshape(group_rows, width)
+            back = lax.dot_general(x, wd[at, :], (((1,), (1,)), ((), ())), preferred_element_type=F32)
+            return acc + jnp.sum(back * hid_ref[p, :, at].astype(F32), axis=1, keepdims=True)
+
+        dots = lax.fori_loop(0, ff // step, inner, jnp.zeros((group_rows, 1), F32))
         for j in range(2):
             s = 2 * p + j
-            spread = jnp.where(meta[s, me, 0:1, :] == slot_iota, meta[s, me, 1:2, :], 0.0)
-            scale = jnp.sum(spread, axis=1, keepdims=True)
-            block = pk[1, s]
-            cpk_ref[s] = block
-            ups_ref[s] = (scale * block.astype(F32)).astype(BF16)
+            hit = meta[s, me, 0:1, :] == slot_iota
+            scale = jnp.sum(jnp.where(hit, meta[s, me, 1:2, :], 0.0), axis=1, keepdims=True)
+            ups_ref[s] = (scale * pk[1, s].astype(F32)).astype(BF16)
+            dots_ref[s] = jnp.sum(
+                jnp.where(hit, dots[j * cap:(j + 1) * cap], 0.0), axis=0, keepdims=True)
 
     for i in range(1, n):
         meta_copy(lax.rem(me + i, n)).start()
     own_sends(0)
+    own_sends(1)
     for i in range(1, n):
         meta_arrive(lax.rem(me + i, n)).wait_recv()
-    for s in range(n):
-        pos_ref[s] = meta[s, me, 0:1, :]
-
-    for g in range(1, pairs):
+
+    others = range(1, pairs)
+    for g in others:
         for c in range(nc - 1):
             relay(0, g, c)
-    for load in loads:
+    for load in loads[:2]:
         load.wait()
     arrived(0, 0)
     products(0)
+    for g in others:
+        relay(0, g, nc - 1)
     sums(0)
-    for g in range(1, pairs):
-        relay(0, g, nc - 1)
-    own_sent(0)
-    own_sends(1)
     activate(0)
-    forward(0)
-    for g in range(1, pairs):
+    for g in others:
         arrived(0, g)
         products(g)
+        if g == 1:
+            forward(0)
         sums(g)
+    for g in others:
+        relay(1, g, 0)
     finish(0)
-    for g in range(1, pairs):
-        for c in range(nc - 1):
+    for g in others:
+        activate(g)
+    for g in others:
+        if nc > 2:
+            relay(1, g, 1)
+    for g in others:
+        forward(g)
+    for g in others:
+        for c in range(2, nc - 1):
             relay(1, g, c)
-    for g in range(1, pairs):
-        activate(g)
-    for g in range(1, pairs):
-        forward(g)
-    for g in range(1, pairs):
+    for g in others:
         finish(g)
+    loads[2].wait()
     arrived(1, 0)
     upstream(0)
-    for g in range(1, pairs):
-        relay(1, g, nc - 1)
-    for g in range(1, pairs):
+    for g in others:
+        if nc > 1:
+            relay(1, g, nc - 1)
+    for g in others:
         arrived(1, g)
         upstream(g)
 
     for i in range(1, n):
         meta_copy(lax.rem(me + i, n)).wait_send()
+    own_sent(0)
     own_sent(1)
     for g in range(pairs):
         s1_copy(g).wait_send()
@@ -312,11 +322,9 @@
                             pack_copy(a, 2 * p + j, c).wait_send()
 
 
-def gradient_kernel(n, cap, tile, hid_ref, ups_ref, cpk_ref, pos_ref, wd_ref, delta_ref,
-                    grad_ref, stat_ref, dots):
-    step = pl.program_id(0)
-    h = hid_ref[...]
-    grad = lax.dot_general(h, ups_ref[...], (((0,), (0,)), ((), ())), preferred_element_type=F32)
+def gradient_kernel(tile, hid_ref, ups_ref, delta_ref, grad_ref, sal_ref):
+    grad = lax.dot_general(hid_ref[...], ups_ref[...], (((0,), (0,)), ((), ())),
+                           preferred_element_type=F32)
     grad_ref[0] = grad
     term = grad * delta_ref[0].astype(F32)
     term = term * term
@@ -324,85 +332,77 @@
     for i in range(1, term.shape[1] // 128):
         lanes = lanes + term[:, i * 128:(i + 1) * 128]
     for i in range(tile // 128):
-        stat_ref[n + step * (tile // 128) + i] = jnp.sum(
-            lanes[i * 128:(i + 1) * 128, :].T, axis=0, keepdims=True)
-    back = lax.dot_general(cpk_ref[...], wd_ref[0], (((1,), (1,)), ((), ())), preferred_element_type=F32)
-    inner = jnp.sum(back * h.astype(F32), axis=1, keepdims=True)
-
-    @pl.when(step == 0)
-    def _():
-        dots[...] = inner
-
-    @pl.when(step > 0)
-    def _():
-        dots[...] += inner
-
-    @pl.when(step == pl.num_programs(0) - 1)
-    def _():
-        slot = lax.broadcasted_iota(jnp.int32, (cap, 128), 0).astype(F32)
-        for s in range(n):
-            mine = jnp.where(pos_ref[s] == slot, dots[s * cap:(s + 1) * cap, :], 0.0)
-            stat_ref[s] = jnp.sum(mine, axis=0, keepdims=True)
-
-
-def reduce_kernel(n, ndp, features, stat_ref, ids_ref, unit_ref, route_ref,
-                  got, total, back, gs, gr, bs, br):
+        sal_ref[i] = jnp.sum(lanes[i * 128:(i + 1) * 128, :].T, axis=0, keepdims=True)
+
+
+def reduce_kernel(n, ndp, features, dots_ref, sal_ref, ids_ref, unit_ref, route_ref,
+                  got, sums, rs, rr, ss, sr):
     me, d, t = lax.axis_index("exp"), lax.axis_index("dp"), lax.axis_index("tp")
     own = d * 2 + t
     peers = 2 * ndp
+    units = unit_ref.shape[0]
     barrier = pltpu.get_barrier_semaphore()
-
-    def peer(i):
-        to = lax.rem(own + i, peers)
-        return to, {"dp": to // 2, "tp": lax.rem(to, 2)}
-
-    for i in range(1, peers):
-        pl.semaphore_signal(barrier, inc=1, device_id=peer(i)[1], device_id_type=MESH)
-    for i in range(1, n):
-        pl.semaphore_signal(barrier, inc=1, device_id={"exp": lax.rem(me + i, n)}, device_id_type=MESH)
-    pl.semaphore_wait(barrier, peers - 1 + n - 1)
-
-    def gather(i):
-        to, where = peer(i)
-        return remote(stat_ref, got.at[own], gs.at[to], gr.at[own], **where)
-
-    def gathered(i):
-        frm, where = peer(i)
-        return remote(stat_ref, got.at[frm], gs.at[frm], gr.at[frm], **where)
-
-    for i in range(1, peers):
-        gather(i).start()
-    got[own] = stat_ref[...]
-    for i in range(1, peers):
-        gathered(i).wait_recv()
-    added = got[0]
-    for i in range(1, peers):
-        added = added + got[i]
-    total[...] = added
-
-    def give(to):
-        return remote(total.at[to], back.at[me], bs.at[to], br.at[me], exp=to)
-
-    def given(frm):
-        return remote(total.at[frm], back.at[frm], bs.at[frm], br.at[frm], exp=frm)
-
-    for i in range(1, n):
-        give(lax.rem(me + i, n)).start()
-    back[me] = total[me]
-    units = unit_ref.shape[0]
-    unit_ref[...] = jnp.log(total[pl.ds(n + own * units, units)] / features + 1e-6)
-    for i in range(1, n):
-        given(lax.rem(me + i, n)).wait_recv()
+    hops = [(i, j) for i in range(n) for j in range(peers) if i or j]
+
+    def there(i, j):
+        e, o = lax.rem(me + i, n), lax.rem(own + j, peers)
+        return e, o, {"exp": e, "dp": o // 2, "tp": lax.rem(o, 2)}
+
+    for i, j in hops:
+        pl.semaphore_signal(barrier, inc=1, device_id=there(i, j)[2], device_id_type=MESH)
+    pl.semaphore_wait(barrier, len(hops))
+
+    def slice_copy(j):
+        e, o, where = there(0, j)
+        return remote(sal_ref.at[pl.ds(o * units, units)], sums.at[own], ss.at[o], sr.at[own], **where)
+
+    def slice_arrive(j):
+        e, o, where = there(0, j)
+        return remote(sal_ref.at[pl.ds(o * units, units)], sums.at[o], ss.at[o], sr.at[o], **where)
+
+    def row_copy(i, j):
+        e, o, where = there(i, j)
+        return remote(dots_ref.at[e], got.at[me, own], rs.at[e, o], rr.at[me, own], **where)
+
+    def row_arrive(i, j):
+        e, o, where = there(i, j)
+        return remote(dots_ref.at[e], got.at[e, o], rs.at[e, o], rr.at[e, o], **where)
+
+    for j in range(1, peers):
+        slice_copy(j).start()
+    for i, j in hops:
+        row_copy(i, j).start()
+    sums[own] = sal_ref[pl.ds(own * units, units)]
+    got[me, own] = dots_ref[me]
+    for j in range(1, peers):
+        slice_arrive(j).wait_recv()
+    total = sums[0]
+    for j in range(1, peers):
+        total = total + sums[j]
+    unit_ref[...] = jnp.log(total / features + 1e-6)
+    for i, j in hops:
+        row_arrive(i, j).wait_recv()
+    rows = []
+    for e in range(n):
+        row = got[e, 0]
+        for j in range(1, peers):
+            row = row + got[e, j]
+        rows.append(row)
     for k in range(ids_ref.shape[0]):
         chosen = ids_ref[k:k + 1, :]
         picked = jnp.zeros(chosen.shape, F32)
         for e in range(n):
-            picked = picked + jnp.where(chosen == e, back[e], 0.0)
+            picked = picked + jnp.where(chosen == e, rows[e], 0.0)
         route_ref[k:k + 1, :] = picked
-    for i in range(1, peers):
-        gather(i).wait_send()
-    for i in range(1, n):
-        give(lax.rem(me + i, n)).wait_send()
+    for j in range(1, peers):
+        slice_copy(j).wait_send()
+    for i, j in hops:
+        row_copy(i, j).wait_send()
+
+
+def hand_over(unit_in, route_in, unit_ref, route_ref):
+    unit_ref[...] = unit_in[...]
+    route_ref[...] = route_in[...]
 
 
 def shards(tokens, cotangent, expert_ids, route_weights, gate_weight, up_weight, down_weight, delta):
@@ -414,23 +414,27 @@
     ff = gate_weight.shape[2]
     half, pairs = ff // 2, n // 2
     part = half // ndp
-    nc = 2 if width % 256 == 0 else 1
+    blocks = width // 256 if width % 256 == 0 else 1
+    unit = width // blocks
+    cuts = (0, 2, 4, 6, 7) if blocks == 7 else (0, blocks)
+    edges = tuple(c * unit for c in cuts)
+    nc = len(edges) - 1
     ids = expert_ids.T
-    shares = route_weights.T.astype(F32)
+    shares = route_weights.T
     dma = pltpu.SemaphoreType.DMA
-    hidden, cpk, ups, pos = pl.pallas_call(
-        functools.partial(exchange_kernel, n, ndp, nc, cap),
+    hidden, ups, dots = pl.pallas_call(
+        functools.partial(exchange_kernel, n, ndp, edges, cap),
         out_shape=(
             jax.ShapeDtypeStruct((pairs, 2 * cap, ff), BF16),
             jax.ShapeDtypeStruct((n, cap, width), BF16),
-            jax.ShapeDtypeStruct((n, cap, width), BF16),
             jax.ShapeDtypeStruct((n, 1, rows), F32),
         ),
-        in_specs=[VMEM, VMEM, VMEM, VMEM, HBM, HBM],
-        out_specs=(VMEM, VMEM, VMEM, VMEM),
+        in_specs=[VMEM, VMEM, VMEM, VMEM, HBM, HBM, HBM],
+        out_specs=(VMEM, VMEM, VMEM),
         scratch_shapes=[
             pltpu.VMEM((width, ff), BF16),
             pltpu.VMEM((width, ff), BF16),
+            pltpu.VMEM((ff, width), BF16),
             pltpu.VMEM((n, n, 8, rows), F32),
             pltpu.VMEM((2, n, rows, width), BF16),
             pltpu.VMEM((2, n, cap, width), BF16),
@@ -442,7 +446,7 @@
             pltpu.VMEM((pairs, ndp, 2, 2 * cap, part), BF16),
             pltpu.VMEM((pairs, 2, 2 * cap, part), F32),
             pltpu.VMEM((pairs, 2, ndp, 2 * cap, part), BF16),
-            dma((2,)), dma((n,)), dma((n,)),
+            dma((3,)), dma((n,)), dma((n,)),
             dma((2, pairs, nc)), dma((2, n, nc)), dma((2, n, nc)), dma((2, n, nc)),
             dma((pairs,)), dma((pairs,)),
             dma((pairs, ndp)), dma((pairs, ndp)),
@@ -452,54 +456,58 @@
         compiler_params=pltpu.CompilerParams(
             collective_id=0, has_side_effects=True, vmem_limit_bytes=60 * 2**20),
         name="exchange",
-    )(ids, shares, tokens, cotangent, gate_weight, up_weight)
-
-    tile = 256
-    stats = n + ff // 128
-    whole = lambda shape: pl.BlockSpec(shape, lambda i: (0,) * len(shape))
-    grad, stat = pl.pallas_call(
-        functools.partial(gradient_kernel, n, cap, tile),
+    )(ids, shares, tokens, cotangent, gate_weight, up_weight, down_weight)
+
+    tile = 512
+    chunks = ff // 128
+    grad, sal = pl.pallas_call(
+        functools.partial(gradient_kernel, tile),
         grid=(ff // tile,),
         out_shape=(
             jax.ShapeDtypeStruct((1, ff, width), F32),
-            jax.ShapeDtypeStruct((stats, 1, 128), F32),
+            jax.ShapeDtypeStruct((chunks, 1, 128), F32),
         ),
         in_specs=[
             pl.BlockSpec((total, tile), lambda i: (0, i)),
-            whole((total, width)),
-            whole((total, width)),
-            whole((n, 1, rows)),
-            pl.BlockSpec((1, tile, width), lambda i: (0, i, 0)),
+            pl.BlockSpec((total, width), lambda i: (0, 0)),
             pl.BlockSpec((1, tile, width), lambda i: (0, i, 0)),
         ],
         out_specs=(
             pl.BlockSpec((1, tile, width), lambda i: (0, i, 0)),
-            whole((stats, 1, 128)),
-        ),
-        scratch_shapes=[pltpu.VMEM((total, 1), F32)],
+            pl.BlockSpec((tile // 128, 1, 128), lambda i: (i, 0, 0)),
+        ),
         compiler_params=pltpu.CompilerParams(vmem_limit_bytes=56 * 2**20),
         name="gradient",
-    )(hidden.reshape(total, ff), ups.reshape(total, width), cpk.reshape(total, width),
-      pos, down_weight, delta)
-
-    units = ff // (2 * ndp) // 128
+    )(hidden.reshape(total, ff), ups.reshape(total, width), delta)
+
+    peers = 2 * ndp
+    units = chunks // peers
     unit, route = pl.pallas_call(
-        functools.partial(reduce_kernel, n, ndp, float(width * 2 * ndp)),
+        functools.partial(reduce_kernel, n, ndp, float(width * peers)),
         out_shape=(
             jax.ShapeDtypeStruct((units, 1, 128), F32),
             jax.ShapeDtypeStruct((chosen, rows), F32),
         ),
-        in_specs=[VMEM, VMEM],
+        in_specs=[VMEM, VMEM, VMEM],
         out_specs=(VMEM, VMEM),
         scratch_shapes=[
-            pltpu.VMEM((2 * ndp, stats, 1, 128), F32),
-            pltpu.VMEM((stats, 1, 128), F32),
-            pltpu.VMEM((n, 1, 128), F32),
-            dma((2 * ndp,)), dma((2 * ndp,)), dma((n,)), dma((n,)),
+            pltpu.VMEM((n, peers, 1, 128), F32),
+            pltpu.VMEM((peers, units, 1, 128), F32),
+            dma((n, peers)), dma((n, peers)), dma((peers,)), dma((peers,)),
         ],
         compiler_params=pltpu.CompilerParams(collective_id=1, has_side_effects=True),
         name="reduce",
-    )(stat, ids)
+    )(dots, sal, ids)
+    unit, route = pl.pallas_call(
+        hand_over,
+        out_shape=(
+            jax.ShapeDtypeStruct(unit.shape, F32),
+            jax.ShapeDtypeStruct(route.shape, F32),
+        ),
+        in_specs=[VMEM, VMEM],
+        out_specs=(VMEM, VMEM),
+        name="hand_over",
+    )(unit, route)
     return grad, unit.reshape(1, units * 128), route.T
 
 

time: 95.3 us -> 87.8 us (0.921)
  Pallas kernels: 90.7 us -> 86.9 us
  local copies, waits for them, and re-layouts: 2.43 us -> 0 us
  other arithmetic: 1.22 us -> 0 us
    pallas_call x3 -> x4, Pallas kernels: 90.7 us -> 86.9 us  [the longest x1 71.5 us: shards(): pl.pallas_call(functools.partial(exchange_kernel, n, ndp, edges, cap), ou...]
    unnamed x2 -> x0, local copies, waits for them, and re-layouts: 2.43 us -> none
    convert_element_type x1 -> x0, other arithmetic: 1.22 us -> none  [shards(): shares = route_weights.T.astype(F32)]
where the time goes in v2:
time: 87.8 us; the launch traced here: 87.6 us
  Pallas kernels  86.9 us (99%)
    pallas_call x1, Pallas kernels, shards(): pl.pallas_call(functools.partial(exchange_kernel, n, ndp, edges, cap), ou...  71.5 us
    pallas_call x1, Pallas kernels, shards(): pl.pallas_call(functools.partial(reduce_kernel, n, ndp, float(width * pee...  7.9 us
    pallas_call x1, Pallas kernels, shards(): pl.pallas_call(functools.partial(gradient_kernel, tile), grid=(ff // tile...  6.33 us

profile of v2, /device:TPU:0, one launch (start us, length us, event | category | flops | bytes accessed | tf_op | source)
XLA Modules:
  0.0 87.6 jit_solution(9345454688655968425)
XLA Ops:
  0.6 71.5 %exchange.1 = (bf16[2,192,1024]{2,1,0:T(8,128)(2,1)}, bf16[4,96,1792]{2,1,0:T(8,128)(2,1)}, f32[4,1,128]{2,1,0:T(1,128)}) custom-call(s32[2,128]{1,0:T(2,128)} %bitcast.8, bf16[2,128]{1,0:T(2,128)(2,1)} %bitcast.10, bf16[128,1792]{1,0:T(8,128)(2,1)} %tok_ref.1, bf16[128,1792]{1,0:T(8,128)(2,1)} %cot_ref.1, bf16[1,1792,1024]{2,1,0:T(8,128)(2,1)} %wg_hbm.1, ...), custom_call_target="tpu_custom_call" | custom-call | tf_op jit(solution)/shard_map/exchange/pallas_call | solution.py:425
  72.1 6.3 %gradient.1 = (f32[1,1024,1792]{2,1,0:T(8,128)}, f32[8,1,128]{2,1,0:T(1,128)}) custom-call(bf16[384,1024]{1,0:T(8,128)(2,1)} %bitcast.7, bf16[384,1792]{1,0:T(8,128)(2,1)} %bitcast.6, bf16[1,1024,1792]{2,1,0:T(8,128)(2,1)} %delta_ref.1), custom_call_target="tpu_custom_call" | custom-call | tf_op jit(solution)/shard_map/gradient/pallas_call | solution.py:463
  78.5 7.9 %reduce.1 = (f32[2,1,128]{2,1,0:T(1,128)}, f32[2,128]{1,0:T(2,128)}) custom-call(f32[4,1,128]{2,1,0:T(1,128)} %get-tuple-element.15.dots_ref, f32[8,1,128]{2,1,0:T(1,128)} %get-tuple-element.16.sal_ref, s32[2,128]{1,0:T(2,128)} %bitcast.9), custom_call_target="tpu_custom_call" | custom-call | tf_op jit(solution)/shard_map/reduce/pallas_call | solution.py:485
  86.4 1.2 %hand_over.1 = (f32[2,1,128]{2,1,0:T(1,128)}, f32[2,128]{1,0:T(2,128)}) custom-call(f32[2,1,128]{2,1,0:T(1,128)} %get-tuple-element.17.unit_in, f32[2,128]{1,0:T(2,128)} %get-tuple-element.18.route_in), custom_call_target="tpu_custom_call" | custom-call | tf_op jit(solution)/shard_map/hand_over/pallas_call | solution.py:501
